TPU v7x, 512 devices: a whole 4x4x16 slice. The times are simulated.
512 devices in a mesh: seq: 32 (over z, core), head: 16 (over y, x).
Axes of the slice: x: 4, y: 4, z: 16, core: 2. Of those that a mesh axis runs over, the one named last changes fastest.
Arguments:
- query_in: bfloat16 [65536, 2048], P(('seq', 'head')), may hold values from -4.6 to 4.6
- key_in: bfloat16 [65536, 2048], P(('seq', 'head')), may hold values from -4.6 to 4.6
- value_in: bfloat16 [65536, 2048], P(('seq', 'head')), may hold values from -6 to 6
- grad_out: bfloat16 [65536, 2048], P(('seq', 'head')), may hold values from -6 to 6
- module_lengths: int32 [512], replicated, may hold values from 1 to 256, 65536 in all
Outputs:
- attn_out: bfloat16 [65536, 2048], P(('seq', 'head'))
- grad_query: bfloat16 [65536, 2048], P(('seq', 'head'))
- grad_key: bfloat16 [65536, 2048], P(('seq', 'head'))
- grad_value: bfloat16 [65536, 2048], P(('seq', 'head'))
Inputs may be any that keep to these rules, and one draw needn't show every extreme that they name: `module_lengths`: the lengths sum to 65536; the longest is exactly 256.
All inputs are finite; a program needn't handle non-finite values.
Results may differ from a plain program's by a relative error of at most 0.03.
Values may be sent and summed in bfloat16 or wider, within the bound.
A program may use at most 64 MiB of HBM per device.

v0:
```python
import math
import jax
import jax.numpy as jnp
from jax import lax
from jax.sharding import PartitionSpec as P

HEAD_DIM = 128


def shifted(value, axis, by):
    peers = lax.axis_size(axis)
    pairs = [(i, i + by) for i in range(peers) if 0 <= i + by < peers]
    return lax.ppermute(value, axis, pairs)


def module_ids(module_lengths, positions):
    module_ends = jnp.cumsum(module_lengths)
    counted = jnp.sum((positions[:, None] >= module_ends[None, :]).astype(jnp.int32), axis=1)
    return jnp.where(positions >= 0, counted, -1)


def allowed_pairs(module_lengths, query_pos, key_pos):
    same = (
        module_ids(module_lengths, query_pos)[:, None]
        == module_ids(module_lengths, key_pos)[None, :]
    )
    return same & (key_pos[None, :] <= query_pos[:, None])


def score_grads(grad_rows, value_block, weights, row_delta, score_scale):
    dprobs = jnp.einsum("qd,kd->qk", grad_rows, value_block, preferred_element_type=jnp.float32)
    return (weights * (dprobs - row_delta[:, None]) * score_scale).astype(jnp.bfloat16)


def key_terms(dscores, weight_bf, query_rows, grad_rows):
    key_grad = jnp.einsum("qk,qd->kd", dscores, query_rows, preferred_element_type=jnp.float32)
    value_grad = jnp.einsum("qk,qd->kd", weight_bf, grad_rows, preferred_element_type=jnp.float32)
    return (key_grad, value_grad)


def one_block(query_rows, key_block, value_block, grad_rows, allowed, score_scale):
    scores = (
        jnp.einsum("qd,kd->qk", query_rows, key_block, preferred_element_type=jnp.float32)
        * score_scale
    )
    row_top = jnp.max(jnp.where(allowed, scores, -jnp.inf), axis=1, keepdims=True)
    row_total = jnp.sum(jnp.where(allowed, jnp.exp(scores - row_top), 0.0), axis=1, keepdims=True)
    log_total = row_top + jnp.log(row_total)
    weights = jnp.where(allowed, jnp.exp(scores - log_total), 0.0)
    weight_bf = weights.astype(jnp.bfloat16)
    attn_rows = jnp.einsum(
        "qk,kd->qd", weight_bf, value_block, preferred_element_type=jnp.float32
    ).astype(jnp.bfloat16)
    row_delta = jnp.sum(grad_rows.astype(jnp.float32) * attn_rows.astype(jnp.float32), axis=1)
    dscores = score_grads(grad_rows, value_block, weights, row_delta, score_scale)
    grad_q = jnp.einsum("qk,kd->qd", dscores, key_block, preferred_element_type=jnp.float32).astype(
        jnp.bfloat16
    )
    key_grad, value_grad = key_terms(dscores, weight_bf, query_rows, grad_rows)
    return (attn_rows, grad_q, key_grad, value_grad, log_total[:, 0], row_delta)


def shards(query_in, key_in, value_in, grad_out, module_lengths):
    head_q, head_k, head_v, head_do = (
        lax.all_to_all(query_in, "head", split_axis=1, concat_axis=0, tiled=True),
        lax.all_to_all(key_in, "head", split_axis=1, concat_axis=0, tiled=True),
        lax.all_to_all(value_in, "head", split_axis=1, concat_axis=0, tiled=True),
        lax.all_to_all(grad_out, "head", split_axis=1, concat_axis=0, tiled=True),
    )
    row_count = head_q.shape[0]
    width = head_q.shape[1]
    local_heads = width // HEAD_DIM
    prior_rows = row_count // 8
    score_scale = HEAD_DIM ** (-0.5)
    tail_start = row_count - prior_rows
    prior_k, prior_v = shifted((head_k[tail_start:], head_v[tail_start:]), "seq", 1)
    row_start = lax.axis_index("seq") * row_count
    query_pos = row_start + jnp.arange(row_count, dtype=jnp.int32)
    before_pos = row_start - prior_rows + jnp.arange(prior_rows, dtype=jnp.int32)
    key_pos = jnp.concatenate([before_pos, query_pos])
    block_rows = math.gcd(row_count, 512)
    block_count = row_count // block_rows
    pos_blocks = query_pos.reshape(block_count, block_rows)

    def by_head(flat, rows):
        return jnp.moveaxis(flat.reshape(rows, local_heads, HEAD_DIM), 1, 0)

    def to_flat(stacked):
        return jnp.moveaxis(stacked, 0, 1).reshape(stacked.shape[1], width)

    query_h = by_head(head_q, row_count)
    grad_h = by_head(head_do, row_count)
    key_h = by_head(jnp.concatenate([prior_k, head_k], axis=0), row_count + prior_rows)
    value_h = by_head(jnp.concatenate([prior_v, head_v], axis=0), row_count + prior_rows)

    def run_head(packed):
        query_rows, key_block, value_block, grad_rows = packed
        query_blocks = query_rows.reshape(block_count, block_rows, HEAD_DIM)
        grad_blocks = grad_rows.reshape(block_count, block_rows, HEAD_DIM)

        def run_block(inner):
            query_part, grad_part, pos_part = inner
            allowed = allowed_pairs(module_lengths, pos_part, key_pos)
            return one_block(query_part, key_block, value_block, grad_part, allowed, score_scale)

        attn_b, grad_qb, key_b, value_b, lse_b, delta_b = lax.map(
            run_block, (query_blocks, grad_blocks, pos_blocks)
        )
        return (
            attn_b.reshape(row_count, HEAD_DIM),
            grad_qb.reshape(row_count, HEAD_DIM),
            jnp.sum(key_b, axis=0),
            jnp.sum(value_b, axis=0),
            lse_b.reshape(row_count),
            delta_b.reshape(row_count),
        )

    attn_h, grad_qh, key_grad, value_grad, log_total, row_delta = lax.map(
        run_head, (query_h, key_h, value_h, grad_h)
    )
    attn_flat = to_flat(attn_h)
    attn_back = lax.all_to_all(attn_flat, "head", split_axis=0, concat_axis=1, tiled=True)
    grad_q = to_flat(grad_qh)
    later_k, later_v = shifted((key_grad[:, :prior_rows], value_grad[:, :prior_rows]), "seq", -1)
    key_total = key_grad[:, prior_rows:].at[:, tail_start:].add(later_k)
    value_total = value_grad[:, prior_rows:].at[:, tail_start:].add(later_v)
    grad_k = to_flat(key_total.astype(jnp.bfloat16))
    grad_v = to_flat(value_total.astype(jnp.bfloat16))
    back_q, back_k, back_v = (
        lax.all_to_all(grad_q, "head", split_axis=0, concat_axis=1, tiled=True),
        lax.all_to_all(grad_k, "head", split_axis=0, concat_axis=1, tiled=True),
        lax.all_to_all(grad_v, "head", split_axis=0, concat_axis=1, tiled=True),
    )
    return (attn_back, back_q, back_k, back_v)


def solution(mesh):
    placed = (
        P(("seq", "head"), None),
        P(("seq", "head"), None),
        P(("seq", "head"), None),
        P(("seq", "head"), None),
        P(),
    )
    return jax.shard_map(
        shards,
        mesh=mesh,
        in_specs=placed,
        out_specs=(
            P(("seq", "head"), None),
            P(("seq", "head"), None),
            P(("seq", "head"), None),
            P(("seq", "head"), None),
        ),
        check_vma=False,
    )
```

profile of v0, /device:TPU:225, one launch (start us, length us, event | category | flops | bytes accessed | tf_op | source)
XLA Modules:
  0.0 204.6 jit_solution(12996659685108868162)
XLA Ops:
  2.6 6.8 %all-to-all-start.1 = ((bf16[128,16,128]{2,0,1:T(8,128)(2,1)}), bf16[128,16,128]{2,0,1:T(8,128)(2,1)S(1)}, u32[]{:S(2)}, u32[]{:S(2)}) async-start(bf16[128,16,128]{2,0,1:T(8,128)(2,1)} %copy_bitcast_fusion.1), calls=%async_computation.1 | async-start | bytes 1048576 | tf_op jit(solution)/shard_map/all_to_all | solution.py:66
  9.4 2.0 copy_bitcast_fusion
  11.3 8.5 %all-to-all-done.1 = bf16[128,16,128]{2,0,1:T(8,128)(2,1)S(1)} async-done(((bf16[128,16,128]{2,0,1:T(8,128)(2,1)}), bf16[128,16,128]{2,0,1:T(8,128)(2,1)S(1)}, u32[]{:S(2)}, u32[]{:S(2)}) %all-to-all-start.1) | async-done | bytes 524320 | tf_op jit(solution)/shard_map/all_to_all | solution.py:66
  19.9 3.6 %all-to-all-start.2 = ((bf16[128,16,128]{2,0,1:T(8,128)(2,1)}), bf16[128,16,128]{2,0,1:T(8,128)(2,1)S(1)}, u32[]{:S(2)}, u32[]{:S(2)}) async-start(bf16[128,16,128]{2,0,1:T(8,128)(2,1)} %copy_bitcast_fusion), calls=%async_computation.2 | async-start | bytes 1048576 | tf_op jit(solution)/shard_map/all_to_all | solution.py:67
  23.5 2.0 copy.74
  25.5 7.6 %all-to-all-done.2 = bf16[128,16,128]{2,0,1:T(8,128)(2,1)S(1)} async-done(((bf16[128,16,128]{2,0,1:T(8,128)(2,1)}), bf16[128,16,128]{2,0,1:T(8,128)(2,1)S(1)}, u32[]{:S(2)}, u32[]{:S(2)}) %all-to-all-start.2) | async-done | bytes 524320 | tf_op jit(solution)/shard_map/all_to_all | solution.py:67
  33.1 3.6 %all-to-all-start.3 = ((bf16[128,16,128]{0,2,1:T(8,128)(2,1)}), bf16[128,16,128]{0,2,1:T(8,128)(2,1)S(1)}, u32[]{:S(2)}, u32[]{:S(2)}) async-start(bf16[128,16,128]{0,2,1:T(8,128)(2,1)} %bitcast.18), calls=%async_computation.3 | async-start | bytes 1048576 | tf_op jit(solution)/shard_map/all_to_all | solution.py:68
  38.2 7.5 %collective-permute-start = (bf16[256,128]{1,0:T(8,128)(2,1)S(1)}, bf16[256,128]{1,0:T(8,128)(2,1)S(1)}, u32[]{:S(2)}, u32[]{:S(2)}) collective-permute-start(bf16[256,128]{1,0:T(8,128)(2,1)S(1)} %bitcast.152), channel_id=1, source_target_pairs={{0,16},{16,32},{32,48},{48,64},{64,80},{80,96},{96,112},{112,128},... | collective-permute-start | bytes 196616 | tf_op jit(solution)/shard_map/ppermute | solution.py:13
  45.7 1.9 collective-permute-start.1
  47.7 6.9 %all-to-all-start = ((bf16[128,16,128]{2,0,1:T(8,128)(2,1)}), bf16[128,16,128]{2,0,1:T(8,128)(2,1)S(1)}, u32[]{:S(2)}, u32[]{:S(2)}) async-start(bf16[128,16,128]{2,0,1:T(8,128)(2,1)} %copy_bitcast_fusion.2), calls=%async_computation | async-start | bytes 1048576 | tf_op jit(solution)/shard_map/all_to_all | solution.py:65
  55.8 9.4 %all-to-all-done = bf16[128,16,128]{2,0,1:T(8,128)(2,1)S(1)} async-done(((bf16[128,16,128]{2,0,1:T(8,128)(2,1)}), bf16[128,16,128]{2,0,1:T(8,128)(2,1)S(1)}, u32[]{:S(2)}, u32[]{:S(2)}) %all-to-all-start) | async-done | bytes 524320 | tf_op jit(solution)/shard_map/all_to_all | solution.py:65
  65.1 74.4 %while.33 = (s32[]{:T(128)}, bf16[4,512,128]{2,1,0:T(8,128)(2,1)}, bf16[4,512,128]{2,1,0:T(8,128)(2,1)}, f32[4,2304,128]{2,1,0:T(8,128)}, f32[4,2304,128]{2,1,0:...) while((s32[]{:T(128)}, bf16[4,512,128]{2,1,0:T(8,128)(2,1)}, ...), condition=%wide.region_8.9_spmd, body=%wide.region_2.8_spmd.sunk | while | flops 1855588608 | bytes 72957736 | solution.py:106
  65.5 1.5 convert_reduce_fusion.4
  68.3 1.7 select_reduce_fusion.5
  70.5 2.7 %fusion.56 = f32[4,2304,128]{2,1,0:T(8,128)} fusion(f32[4,2304,128]{2,1,0:T(8,128)} %get-tuple-element.443, s32[]{:T(128)} %get-tuple-element.439, bf16[1,512,128]{2,1,0:T(8,128)(2,1)S(1)} %constant_dynamic-slice_fusion.4, f32[512,2304]{1,0:T(8,128)S(1)} %get-tuple-element.421, f32[512]{0:T(512)S(1)} %log_add_fusion.2, ...), kind=kOutput, calls=%fused_computation.11.clone.1 | convolution fusion | flops 309067776 | bytes 6054400 | tf_op jit(solution)/shard_map/while/body/eval_jaxpr/while/body/eval_jaxpr/qk,qd->kd/dot_general | solution.py:37
  73.4 3.9 %multiply_reduce_fusion.2 = (f32[512]{0:T(512)S(1)}, bf16[512,128]{0,1:T(8,128)(2,1)S(1)}) fusion(bf16[1,512,128]{1,2,0:T(8,128)(2,1)S(1)} %copy.99, bf16[2304,128]{1,0:T(8,128)(2,1)S(1)} %copy-done.2, f32[512,2304]{1,0:T(8,128)} %copy-done.1, f32[512]{0:T(512)S(1)} %log_add_fusion.2, s32[512]{0:T(512)S(1)} %bitcast.148, ...), kind=kOutput, calls=%fused_computation.20.clone.1 | convolution fusion | flops 309394944 | bytes 5597184 | tf_op jit(solution)/shard_map/while/body/eval_jaxpr/while/body/eval_jaxpr/qk,kd->qd/dot_general | solution.py:51
  77.4 2.3 %fusion.53 = bf16[512,2304]{1,0:T(8,128)(2,1)S(1)} fusion(bf16[2304,128]{1,0:T(8,128)(2,1)S(1)} %copy-done.2, f32[512,2304]{1,0:T(8,128)S(1)} %bitcast.121, f32[512]{0:T(512)S(1)} %get-tuple-element.424, f32[512]{0:T(512)S(1)} %log_add_fusion.2, bf16[1,512,128]{2,1,0:T(8,128)(2,1)S(1)} %constant_dynamic-slice_fusion.4, s32[512]{0:T(512)S(1)} %bitcast.149, ...), kind=kOutput, calls=%fused_computation.9.clone.1 | convolution fusion | flops 312606720 | bytes 7825408 | tf_op jit(solution)/shard_map/while/body/eval_jaxpr/while/body/eval_jaxpr/qd,kd->qk/dot_general | solution.py:31
  79.6 1.8 fusion.55
  84.1 1.5 convert_reduce_fusion.4
  86.9 1.7 select_reduce_fusion.5
  89.1 2.7 %fusion.56 = f32[4,2304,128]{2,1,0:T(8,128)} fusion(f32[4,2304,128]{2,1,0:T(8,128)} %get-tuple-element.443, s32[]{:T(128)} %get-tuple-element.439, bf16[1,512,128]{2,1,0:T(8,128)(2,1)S(1)} %constant_dynamic-slice_fusion.4, f32[512,2304]{1,0:T(8,128)S(1)} %get-tuple-element.421, f32[512]{0:T(512)S(1)} %log_add_fusion.2, ...), kind=kOutput, calls=%fused_computation.11.clone.1 | convolution fusion | flops 309067776 | bytes 6054400 | tf_op jit(solution)/shard_map/while/body/eval_jaxpr/while/body/eval_jaxpr/qk,qd->kd/dot_general | solution.py:37
  92.0 3.9 %multiply_reduce_fusion.2 = (f32[512]{0:T(512)S(1)}, bf16[512,128]{0,1:T(8,128)(2,1)S(1)}) fusion(bf16[1,512,128]{1,2,0:T(8,128)(2,1)S(1)} %copy.99, bf16[2304,128]{1,0:T(8,128)(2,1)S(1)} %copy-done.2, f32[512,2304]{1,0:T(8,128)} %copy-done.1, f32[512]{0:T(512)S(1)} %log_add_fusion.2, s32[512]{0:T(512)S(1)} %bitcast.148, ...), kind=kOutput, calls=%fused_computation.20.clone.1 | convolution fusion | flops 309394944 | bytes 5597184 | tf_op jit(solution)/shard_map/while/body/eval_jaxpr/while/body/eval_jaxpr/qk,kd->qd/dot_general | solution.py:51
  95.9 2.3 %fusion.53 = bf16[512,2304]{1,0:T(8,128)(2,1)S(1)} fusion(bf16[2304,128]{1,0:T(8,128)(2,1)S(1)} %copy-done.2, f32[512,2304]{1,0:T(8,128)S(1)} %bitcast.121, f32[512]{0:T(512)S(1)} %get-tuple-element.424, f32[512]{0:T(512)S(1)} %log_add_fusion.2, bf16[1,512,128]{2,1,0:T(8,128)(2,1)S(1)} %constant_dynamic-slice_fusion.4, s32[512]{0:T(512)S(1)} %bitcast.149, ...), kind=kOutput, calls=%fused_computation.9.clone.1 | convolution fusion | flops 312606720 | bytes 7825408 | tf_op jit(solution)/shard_map/while/body/eval_jaxpr/while/body/eval_jaxpr/qd,kd->qk/dot_general | solution.py:31
  98.2 1.9 fusion.55
  102.7 1.5 convert_reduce_fusion.4
  105.5 1.7 select_reduce_fusion.5
  107.7 2.7 %fusion.56 = f32[4,2304,128]{2,1,0:T(8,128)} fusion(f32[4,2304,128]{2,1,0:T(8,128)} %get-tuple-element.443, s32[]{:T(128)} %get-tuple-element.439, bf16[1,512,128]{2,1,0:T(8,128)(2,1)S(1)} %constant_dynamic-slice_fusion.4, f32[512,2304]{1,0:T(8,128)S(1)} %get-tuple-element.421, f32[512]{0:T(512)S(1)} %log_add_fusion.2, ...), kind=kOutput, calls=%fused_computation.11.clone.1 | convolution fusion | flops 309067776 | bytes 6054400 | tf_op jit(solution)/shard_map/while/body/eval_jaxpr/while/body/eval_jaxpr/qk,qd->kd/dot_general | solution.py:37
  110.6 3.9 %multiply_reduce_fusion.2 = (f32[512]{0:T(512)S(1)}, bf16[512,128]{0,1:T(8,128)(2,1)S(1)}) fusion(bf16[1,512,128]{1,2,0:T(8,128)(2,1)S(1)} %copy.99, bf16[2304,128]{1,0:T(8,128)(2,1)S(1)} %copy-done.2, f32[512,2304]{1,0:T(8,128)} %copy-done.1, f32[512]{0:T(512)S(1)} %log_add_fusion.2, s32[512]{0:T(512)S(1)} %bitcast.148, ...), kind=kOutput, calls=%fused_computation.20.clone.1 | convolution fusion | flops 309394944 | bytes 5597184 | tf_op jit(solution)/shard_map/while/body/eval_jaxpr/while/body/eval_jaxpr/qk,kd->qd/dot_general | solution.py:51
  114.5 2.3 %fusion.53 = bf16[512,2304]{1,0:T(8,128)(2,1)S(1)} fusion(bf16[2304,128]{1,0:T(8,128)(2,1)S(1)} %copy-done.2, f32[512,2304]{1,0:T(8,128)S(1)} %bitcast.121, f32[512]{0:T(512)S(1)} %get-tuple-element.424, f32[512]{0:T(512)S(1)} %log_add_fusion.2, bf16[1,512,128]{2,1,0:T(8,128)(2,1)S(1)} %constant_dynamic-slice_fusion.4, s32[512]{0:T(512)S(1)} %bitcast.149, ...), kind=kOutput, calls=%fused_computation.9.clone.1 | convolution fusion | flops 312606720 | bytes 7825408 | tf_op jit(solution)/shard_map/while/body/eval_jaxpr/while/body/eval_jaxpr/qd,kd->qk/dot_general | solution.py:31
  116.8 1.9 fusion.55
  121.3 1.5 convert_reduce_fusion.4
  124.1 1.7 select_reduce_fusion.5
  126.3 2.8 %fusion.56 = f32[4,2304,128]{2,1,0:T(8,128)} fusion(f32[4,2304,128]{2,1,0:T(8,128)} %get-tuple-element.443, s32[]{:T(128)} %get-tuple-element.439, bf16[1,512,128]{2,1,0:T(8,128)(2,1)S(1)} %constant_dynamic-slice_fusion.4, f32[512,2304]{1,0:T(8,128)S(1)} %get-tuple-element.421, f32[512]{0:T(512)S(1)} %log_add_fusion.2, ...), kind=kOutput, calls=%fused_computation.11.clone.1 | convolution fusion | flops 309067776 | bytes 6054400 | tf_op jit(solution)/shard_map/while/body/eval_jaxpr/while/body/eval_jaxpr/qk,qd->kd/dot_general | solution.py:37
  129.2 3.9 %multiply_reduce_fusion.2 = (f32[512]{0:T(512)S(1)}, bf16[512,128]{0,1:T(8,128)(2,1)S(1)}) fusion(bf16[1,512,128]{1,2,0:T(8,128)(2,1)S(1)} %copy.99, bf16[2304,128]{1,0:T(8,128)(2,1)S(1)} %copy-done.2, f32[512,2304]{1,0:T(8,128)} %copy-done.1, f32[512]{0:T(512)S(1)} %log_add_fusion.2, s32[512]{0:T(512)S(1)} %bitcast.148, ...), kind=kOutput, calls=%fused_computation.20.clone.1 | convolution fusion | flops 309394944 | bytes 5597184 | tf_op jit(solution)/shard_map/while/body/eval_jaxpr/while/body/eval_jaxpr/qk,kd->qd/dot_general | solution.py:51
  133.2 2.3 %fusion.53 = bf16[512,2304]{1,0:T(8,128)(2,1)S(1)} fusion(bf16[2304,128]{1,0:T(8,128)(2,1)S(1)} %copy-done.2, f32[512,2304]{1,0:T(8,128)S(1)} %bitcast.121, f32[512]{0:T(512)S(1)} %get-tuple-element.424, f32[512]{0:T(512)S(1)} %log_add_fusion.2, bf16[1,512,128]{2,1,0:T(8,128)(2,1)S(1)} %constant_dynamic-slice_fusion.4, s32[512]{0:T(512)S(1)} %bitcast.149, ...), kind=kOutput, calls=%fused_computation.9.clone.1 | convolution fusion | flops 312606720 | bytes 7825408 | tf_op jit(solution)/shard_map/while/body/eval_jaxpr/while/body/eval_jaxpr/qd,kd->qk/dot_general | solution.py:31
  135.5 1.8 fusion.55
  139.6 13.3 %all_to_all.146 = bf16[16,128,128]{2,1,0:T(8,128)(2,1)S(1)} all-to-all(bf16[16,128,128]{2,1,0:T(8,128)(2,1)} %bitcast.150), channel_id=1, replica_groups=mesh['seq'=32,'head'=16] {'head'}, dimensions={0} | all-to-all | bytes 1048576 | tf_op jit(solution)/shard_map/all_to_all | solution.py:122
  152.9 3.6 %all-to-all-start.5 = ((bf16[16,128,128]{2,1,0:T(8,128)(2,1)}), bf16[16,128,128]{2,1,0:T(8,128)(2,1)S(1)}, u32[]{:S(2)}, u32[]{:S(2)}) async-start(bf16[16,128,128]{2,1,0:T(8,128)(2,1)} %bitcast.151), calls=%async_computation.5 | async-start | bytes 1048576 | tf_op jit(solution)/shard_map/all_to_all | solution.py:130
  156.5 2.7 %reduce_sum.65 = f32[2304,128]{1,0:T(8,128)S(1)} reduce(f32[4,2304,128]{2,1,0:T(8,128)} %get-tuple-element.213, f32[]{:T(128)} %constant.129.clone.1), dimensions={0}, to_apply=%region_10.11 | reduce | flops 884736 | bytes 5898244 | tf_op jit(solution)/shard_map/while/body/eval_jaxpr/reduce_sum | solution.py:113
  159.2 4.6 %collective-permute-start.3 = (f32[1,256,128]{2,1,0:T(8,128)S(1)}, f32[1,256,128]{2,1,0:T(8,128)S(1)}, u32[]{:S(2)}, u32[]{:S(2)}) collective-permute-start(f32[1,256,128]{2,1,0:T(8,128)S(1)} %slice.103), channel_id=1, source_target_pairs={{16,0},{32,16},{48,32},{64,48},{80,64},{96,80},{112,96},{128,112},... | collective-permute-start | bytes 393224 | tf_op jit(solution)/shard_map/ppermute | solution.py:13
  164.7 2.7 %collective-permute-done.3 = f32[1,256,128]{2,1,0:T(8,128)S(1)} collective-permute-done((f32[1,256,128]{2,1,0:T(8,128)S(1)}, f32[1,256,128]{2,1,0:T(8,128)S(1)}, u32[]{:S(2)}, u32[]{:S(2)}) %collective-permute-start.3) | collective-permute-done | bytes 131104 | tf_op jit(solution)/shard_map/ppermute | solution.py:13
  168.1 6.6 %all-to-all-start.7 = ((bf16[16,128,128]{2,1,0:T(8,128)(2,1)}), bf16[16,128,128]{2,1,0:T(8,128)(2,1)S(1)}, u32[]{:S(2)}, u32[]{:S(2)}) async-start(bf16[16,128,128]{2,1,0:T(8,128)(2,1)} %bitcast.32), calls=%async_computation.7 | async-start | bytes 1048576 | tf_op jit(solution)/shard_map/all_to_all | solution.py:132
  174.6 2.7 %reduce_sum.64 = f32[2304,128]{1,0:T(8,128)S(1)} reduce(f32[4,2304,128]{2,1,0:T(8,128)} %get-tuple-element.212, f32[]{:T(128)} %constant.129.clone.1), dimensions={0}, to_apply=%region_9.10 | reduce | flops 884736 | bytes 5898244 | tf_op jit(solution)/shard_map/while/body/eval_jaxpr/reduce_sum | solution.py:112
  177.4 1.9 collective-permute-start.2
  180.2 4.7 %collective-permute-done.2 = f32[1,256,128]{2,1,0:T(8,128)S(1)} collective-permute-done((f32[1,256,128]{2,1,0:T(8,128)S(1)}, f32[1,256,128]{2,1,0:T(8,128)S(1)}, u32[]{:S(2)}, u32[]{:S(2)}) %collective-permute-start.2) | collective-permute-done | bytes 131104 | tf_op jit(solution)/shard_map/ppermute | solution.py:13
  185.5 1.6 all-to-all-done.7
  187.1 5.1 %all-to-all-start.6 = ((bf16[16,128,128]{2,1,0:T(8,128)(2,1)}), bf16[16,128,128]{2,1,0:T(8,128)(2,1)S(1)}, u32[]{:S(2)}, u32[]{:S(2)}) async-start(bf16[16,128,128]{2,1,0:T(8,128)(2,1)} %bitcast.28), calls=%async_computation.6 | async-start | bytes 1048576 | tf_op jit(solution)/shard_map/all_to_all | solution.py:131
  196.1 7.2 %all-to-all-done.6 = bf16[16,128,128]{2,1,0:T(8,128)(2,1)S(1)} async-done(((bf16[16,128,128]{2,1,0:T(8,128)(2,1)}), bf16[16,128,128]{2,1,0:T(8,128)(2,1)S(1)}, u32[]{:S(2)}, u32[]{:S(2)}) %all-to-all-start.6) | async-done | bytes 524320 | tf_op jit(solution)/shard_map/all_to_all | solution.py:131
  (131 shorter events, 30.7 us)
Async XLA Ops:
  0.6 1.0 copy-start
  0.6 36.1 %copy-start.4 = (s32[512]{0:T(512)S(1)}, s32[512]{0:T(512)}, u32[]{:S(2)}) copy-start(s32[512]{0:T(512)} %param.15) | copy-start | bytes 6148
  1.7 35.6 %copy-start.3 = (bf16[128,2048]{1,0:T(8,128)(2,1)S(1)}, bf16[128,2048]{1,0:T(8,128)(2,1)}, u32[]{:S(2)}) copy-start(bf16[128,2048]{1,0:T(8,128)(2,1)} %param.11) | copy-start | bytes 1572868
  2.6 17.3 %all-to-all-start.1 = ((bf16[128,16,128]{2,0,1:T(8,128)(2,1)}), bf16[128,16,128]{2,0,1:T(8,128)(2,1)S(1)}, u32[]{:S(2)}, u32[]{:S(2)}) async-start(bf16[128,16,128]{2,0,1:T(8,128)(2,1)} %copy_bitcast_fusion.1), calls=%async_computation.1 | async-start | bytes 1048576 | tf_op jit(solution)/shard_map/all_to_all | solution.py:66
  19.9 13.2 %all-to-all-start.2 = ((bf16[128,16,128]{2,0,1:T(8,128)(2,1)}), bf16[128,16,128]{2,0,1:T(8,128)(2,1)S(1)}, u32[]{:S(2)}, u32[]{:S(2)}) async-start(bf16[128,16,128]{2,0,1:T(8,128)(2,1)} %copy_bitcast_fusion), calls=%async_computation.2 | async-start | bytes 1048576 | tf_op jit(solution)/shard_map/all_to_all | solution.py:67
  33.1 14.5 %all-to-all-start.3 = ((bf16[128,16,128]{0,2,1:T(8,128)(2,1)}), bf16[128,16,128]{0,2,1:T(8,128)(2,1)S(1)}, u32[]{:S(2)}, u32[]{:S(2)}) async-start(bf16[128,16,128]{0,2,1:T(8,128)(2,1)} %bitcast.18), calls=%async_computation.3 | async-start | bytes 1048576 | tf_op jit(solution)/shard_map/all_to_all | solution.py:68
  38.2 16.6 %collective-permute-start = (bf16[256,128]{1,0:T(8,128)(2,1)S(1)}, bf16[256,128]{1,0:T(8,128)(2,1)S(1)}, u32[]{:S(2)}, u32[]{:S(2)}) collective-permute-start(bf16[256,128]{1,0:T(8,128)(2,1)S(1)} %bitcast.152), channel_id=1, source_target_pairs={{0,16},{16,32},{32,48},{48,64},{64,80},{80,96},{96,112},{112,128},... | collective-permute-start | bytes 196616 | tf_op jit(solution)/shard_map/ppermute | solution.py:13
  45.7 9.2 %collective-permute-start.1 = (bf16[256,128]{1,0:T(8,128)(2,1)S(1)}, bf16[256,128]{1,0:T(8,128)(2,1)S(1)}, u32[]{:S(2)}, u32[]{:S(2)}) collective-permute-start(bf16[256,128]{1,0:T(8,128)(2,1)S(1)} %bitcast.153), channel_id=1, source_target_pairs={{0,16},{16,32},{32,48},{48,64},{64,80},{80,96},{96,112},{112,128},... | collective-permute-start | bytes 196616 | tf_op jit(solution)/shard_map/ppermute | solution.py:13
  47.7 17.5 %all-to-all-start = ((bf16[128,16,128]{2,0,1:T(8,128)(2,1)}), bf16[128,16,128]{2,0,1:T(8,128)(2,1)S(1)}, u32[]{:S(2)}, u32[]{:S(2)}) async-start(bf16[128,16,128]{2,0,1:T(8,128)(2,1)} %copy_bitcast_fusion.2), calls=%async_computation | async-start | bytes 1048576 | tf_op jit(solution)/shard_map/all_to_all | solution.py:65
  68.3 2.3 %copy-start.1 = (f32[512,2304]{1,0:T(8,128)}, f32[512,2304]{1,0:T(8,128)S(1)}, u32[]{:S(2)}) copy-start(f32[512,2304]{1,0:T(8,128)S(1)} %get-tuple-element.421) | copy-start | bytes 14155780 | tf_op jit(solution)/shard_map/while/body/eval_jaxpr/while
  70.5 2.9 %copy-start.2 = (bf16[2304,128]{1,0:T(8,128)(2,1)S(1)}, bf16[2304,128]{1,0:T(8,128)(2,1)}, u32[]{:S(2)}) copy-start(bf16[2304,128]{1,0:T(8,128)(2,1)} %get-tuple-element.464) | copy-start | bytes 1769476 | tf_op jit(solution)/shard_map/while/body/eval_jaxpr/while
  73.4 4.0 %slice-start = ((s8[4718592]{0:T(1024)(128)(4,1)}), s8[4194304]{0:T(1024)(128)(4,1)S(1)}, s32[]{:S(2)}) async-start(s8[4718592]{0:T(1024)(128)(4,1)} %bitcast.120), calls=%async_computation.8 | async-start | bytes 8388608 | tf_op jit(solution)/shard_map/while/body/eval_jaxpr/while
  73.4 3.9 %slice-start.1 = ((s8[4718592]{0:T(1024)(128)(4,1)}), s8[524288]{0:T(1024)(128)(4,1)S(1)}, s32[]{:S(2)}) async-start(s8[4718592]{0:T(1024)(128)(4,1)} %bitcast.120), calls=%async_computation.9 | async-start | bytes 1048576 | tf_op jit(solution)/shard_map/while/body/eval_jaxpr/while
  86.9 2.3 %copy-start.1 = (f32[512,2304]{1,0:T(8,128)}, f32[512,2304]{1,0:T(8,128)S(1)}, u32[]{:S(2)}) copy-start(f32[512,2304]{1,0:T(8,128)S(1)} %get-tuple-element.421) | copy-start | bytes 14155780 | tf_op jit(solution)/shard_map/while/body/eval_jaxpr/while
  89.1 2.8 %copy-start.2 = (bf16[2304,128]{1,0:T(8,128)(2,1)S(1)}, bf16[2304,128]{1,0:T(8,128)(2,1)}, u32[]{:S(2)}) copy-start(bf16[2304,128]{1,0:T(8,128)(2,1)} %get-tuple-element.464) | copy-start | bytes 1769476 | tf_op jit(solution)/shard_map/while/body/eval_jaxpr/while
  91.9 4.0 %slice-start = ((s8[4718592]{0:T(1024)(128)(4,1)}), s8[4194304]{0:T(1024)(128)(4,1)S(1)}, s32[]{:S(2)}) async-start(s8[4718592]{0:T(1024)(128)(4,1)} %bitcast.120), calls=%async_computation.8 | async-start | bytes 8388608 | tf_op jit(solution)/shard_map/while/body/eval_jaxpr/while
  92.0 3.9 %slice-start.1 = ((s8[4718592]{0:T(1024)(128)(4,1)}), s8[524288]{0:T(1024)(128)(4,1)S(1)}, s32[]{:S(2)}) async-start(s8[4718592]{0:T(1024)(128)(4,1)} %bitcast.120), calls=%async_computation.9 | async-start | bytes 1048576 | tf_op jit(solution)/shard_map/while/body/eval_jaxpr/while
  105.5 2.3 %copy-start.1 = (f32[512,2304]{1,0:T(8,128)}, f32[512,2304]{1,0:T(8,128)S(1)}, u32[]{:S(2)}) copy-start(f32[512,2304]{1,0:T(8,128)S(1)} %get-tuple-element.421) | copy-start | bytes 14155780 | tf_op jit(solution)/shard_map/while/body/eval_jaxpr/while
  107.7 2.8 %copy-start.2 = (bf16[2304,128]{1,0:T(8,128)(2,1)S(1)}, bf16[2304,128]{1,0:T(8,128)(2,1)}, u32[]{:S(2)}) copy-start(bf16[2304,128]{1,0:T(8,128)(2,1)} %get-tuple-element.464) | copy-start | bytes 1769476 | tf_op jit(solution)/shard_map/while/body/eval_jaxpr/while
  110.5 4.0 %slice-start = ((s8[4718592]{0:T(1024)(128)(4,1)}), s8[4194304]{0:T(1024)(128)(4,1)S(1)}, s32[]{:S(2)}) async-start(s8[4718592]{0:T(1024)(128)(4,1)} %bitcast.120), calls=%async_computation.8 | async-start | bytes 8388608 | tf_op jit(solution)/shard_map/while/body/eval_jaxpr/while
  110.6 3.9 %slice-start.1 = ((s8[4718592]{0:T(1024)(128)(4,1)}), s8[524288]{0:T(1024)(128)(4,1)S(1)}, s32[]{:S(2)}) async-start(s8[4718592]{0:T(1024)(128)(4,1)} %bitcast.120), calls=%async_computation.9 | async-start | bytes 1048576 | tf_op jit(solution)/shard_map/while/body/eval_jaxpr/while
  124.1 2.3 %copy-start.1 = (f32[512,2304]{1,0:T(8,128)}, f32[512,2304]{1,0:T(8,128)S(1)}, u32[]{:S(2)}) copy-start(f32[512,2304]{1,0:T(8,128)S(1)} %get-tuple-element.421) | copy-start | bytes 14155780 | tf_op jit(solution)/shard_map/while/body/eval_jaxpr/while
  126.3 2.9 %copy-start.2 = (bf16[2304,128]{1,0:T(8,128)(2,1)S(1)}, bf16[2304,128]{1,0:T(8,128)(2,1)}, u32[]{:S(2)}) copy-start(bf16[2304,128]{1,0:T(8,128)(2,1)} %get-tuple-element.464) | copy-start | bytes 1769476 | tf_op jit(solution)/shard_map/while/body/eval_jaxpr/while
  129.2 4.0 %slice-start = ((s8[4718592]{0:T(1024)(128)(4,1)}), s8[4194304]{0:T(1024)(128)(4,1)S(1)}, s32[]{:S(2)}) async-start(s8[4718592]{0:T(1024)(128)(4,1)} %bitcast.120), calls=%async_computation.8 | async-start | bytes 8388608 | tf_op jit(solution)/shard_map/while/body/eval_jaxpr/while
  129.2 3.9 %slice-start.1 = ((s8[4718592]{0:T(1024)(128)(4,1)}), s8[524288]{0:T(1024)(128)(4,1)S(1)}, s32[]{:S(2)}) async-start(s8[4718592]{0:T(1024)(128)(4,1)} %bitcast.120), calls=%async_computation.9 | async-start | bytes 1048576 | tf_op jit(solution)/shard_map/while/body/eval_jaxpr/while
  152.9 15.2 %all-to-all-start.5 = ((bf16[16,128,128]{2,1,0:T(8,128)(2,1)}), bf16[16,128,128]{2,1,0:T(8,128)(2,1)S(1)}, u32[]{:S(2)}, u32[]{:S(2)}) async-start(bf16[16,128,128]{2,1,0:T(8,128)(2,1)} %bitcast.151), calls=%async_computation.5 | async-start | bytes 1048576 | tf_op jit(solution)/shard_map/all_to_all | solution.py:130
  159.2 8.2 %collective-permute-start.3 = (f32[1,256,128]{2,1,0:T(8,128)S(1)}, f32[1,256,128]{2,1,0:T(8,128)S(1)}, u32[]{:S(2)}, u32[]{:S(2)}) collective-permute-start(f32[1,256,128]{2,1,0:T(8,128)S(1)} %slice.103), channel_id=1, source_target_pairs={{16,0},{32,16},{48,32},{64,48},{80,64},{96,80},{112,96},{128,112},... | collective-permute-start | bytes 393224 | tf_op jit(solution)/shard_map/ppermute | solution.py:13
  168.1 19.1 %all-to-all-start.7 = ((bf16[16,128,128]{2,1,0:T(8,128)(2,1)}), bf16[16,128,128]{2,1,0:T(8,128)(2,1)S(1)}, u32[]{:S(2)}, u32[]{:S(2)}) async-start(bf16[16,128,128]{2,1,0:T(8,128)(2,1)} %bitcast.32), calls=%async_computation.7 | async-start | bytes 1048576 | tf_op jit(solution)/shard_map/all_to_all | solution.py:132
  177.4 7.5 %collective-permute-start.2 = (f32[1,256,128]{2,1,0:T(8,128)S(1)}, f32[1,256,128]{2,1,0:T(8,128)S(1)}, u32[]{:S(2)}, u32[]{:S(2)}) collective-permute-start(f32[1,256,128]{2,1,0:T(8,128)S(1)} %slice.100), channel_id=1, source_target_pairs={{16,0},{32,16},{48,32},{64,48},{80,64},{96,80},{112,96},{128,112},... | collective-permute-start | bytes 393224 | tf_op jit(solution)/shard_map/ppermute | solution.py:13
  187.1 16.2 %all-to-all-start.6 = ((bf16[16,128,128]{2,1,0:T(8,128)(2,1)}), bf16[16,128,128]{2,1,0:T(8,128)(2,1)S(1)}, u32[]{:S(2)}, u32[]{:S(2)}) async-start(bf16[16,128,128]{2,1,0:T(8,128)(2,1)} %bitcast.28), calls=%async_computation.6 | async-start | bytes 1048576 | tf_op jit(solution)/shard_map/all_to_all | solution.py:131
where the time goes:
time: 206 us; the launch traced here: 205 us
  matrix products  53.9 us (26%)
  starting transfers between devices  52 us (25%)
  waiting for transfers between devices  41.8 us (20%)
  other arithmetic  22.4 us (11%)
  local copies, waits for them, and re-layouts  19.9 us (10%)
  blocking collectives  13.3 us (6%)
    ppermute x4, starting transfers between devices, shifted(): return lax.ppermute(value, axis, pairs)  16 us
    dot_general x4, matrix products, one_block(): jnp.einsum('qk,kd->qd', weight_bf, value_block, preferred_element_type=jn...  15.7 us
    all_to_all x1, blocking collectives, shards(): lax.all_to_all(attn_flat, 'head', split_axis=0, concat_axis=1, tiled=True)  13.3 us
    dot_general x4, matrix products, key_terms(): jnp.einsum('qk,qd->kd', weight_bf, grad_rows, preferred_element_type=jnp....  10.9 us
    all_to_all x1, waiting for transfers between devices, shards(): lax.all_to_all(query_in, 'head', split_axis=1, concat_axis=0, tiled=True)  9.36 us
    dot_general x4, matrix products, score_grads(): jnp.einsum('qd,kd->qk', grad_rows, value_block, preferred_element_type=jn...  9.12 us
    all_to_all x1, waiting for transfers between devices, shards(): lax.all_to_all(key_in, 'head', split_axis=1, concat_axis=0, tiled=True)  8.54 us
    all_to_all x1, waiting for transfers between devices, shards(): lax.all_to_all(value_in, 'head', split_axis=1, concat_axis=0, tiled=True)  7.61 us
  transfers between devices with their start and end apart: 11, of which 7 were waited for; matrix products, arithmetic and copies ran while one was open for 9% of the time, Pallas kernels for 0%

commit v1 on v0

--- a/solution.py
+++ b/solution.py
@@ -3,6 +3,7 @@
 import jax.numpy as jnp
 from jax import lax
 from jax.sharding import PartitionSpec as P
+from jax.lax import all_to_all, psum
 
 HEAD_DIM = 128
 
@@ -126,9 +127,22 @@
     value_total = value_grad[:, prior_rows:].at[:, tail_start:].add(later_v)
     grad_k = to_flat(key_total.astype(jnp.bfloat16))
     grad_v = to_flat(value_total.astype(jnp.bfloat16))
+
+    def feed_the_pieces_all(obj, dim_i, axis_k):
+        part_now = jnp.concatenate(
+            all_to_all(
+                jnp.stack(jnp.split(obj, psum(1, axis_name="head"), dim_i), 0),
+                axis_name="head",
+                split_axis=0,
+                concat_axis=0,
+            ),
+            axis_k,
+        )
+        return part_now
+
     back_q, back_k, back_v = (
         lax.all_to_all(grad_q, "head", split_axis=0, concat_axis=1, tiled=True),
-        lax.all_to_all(grad_k, "head", split_axis=0, concat_axis=1, tiled=True),
+        feed_the_pieces_all(grad_k, 0, 1),
         lax.all_to_all(grad_v, "head", split_axis=0, concat_axis=1, tiled=True),
     )
     return (attn_back, back_q, back_k, back_v)

time: 206 us -> 216 us (1.049)
  blocking collectives: 13.3 us -> 0 us
  local copies, waits for them, and re-layouts: 19.9 us -> 29 us
  waiting for transfers between devices: 41.8 us -> 47.9 us
  matrix products: 53.9 us -> 58.4 us
  starting transfers between devices: 52 us -> 55.1 us
    all_to_all x1 -> x0, blocking collectives: 13.3 us -> none  [shards(): lax.all_to_all(attn_flat, 'head', split_axis=0, concat_axis=1, tiled=True)]
    unnamed x11 -> x26, local copies, waits for them, and re-layouts: 7.13 us -> 16.4 us
    all_to_all x1, waiting for transfers between devices: 0.01 us -> 8.45 us  [shards(): lax.all_to_all(grad_q, 'head', split_axis=0, concat_axis=1, tiled=True)]
    all_to_all x1, waiting for transfers between devices: 1.6 us -> 8.36 us  [shards(): lax.all_to_all(grad_v, 'head', split_axis=0, concat_axis=1, tiled=True)]
    ppermute x4, waiting for transfers between devices: 7.43 us -> 3.07 us  [shifted(): return lax.ppermute(value, axis, pairs)]
    dot_general x4, matrix products: 5.07 us -> 9.35 us  [one_block(): jnp.einsum('qd,kd->qk', query_rows, key_block, preferred_element_type=jnp...]
    all_to_all x1 -> x2, waiting for transfers between devices: 7.24 us -> 3.3 us  [the longest x1 3.29 us: shards(): lax.all_to_all(attn_flat, 'head', split_axis=0, concat_axis=1, tiled=True)]
    all_to_all x1 -> x2, starting transfers between devices: 5.06 us -> 7.16 us  [the longest x1 3.59 us: shards(): lax.all_to_all(attn_flat, 'head', split_axis=0, concat_axis=1, tiled=True)]
  transfers between devices with their start and end apart: 11 -> 12, of which waited for: 7 -> 7; matrix products, arithmetic and copies ran while one was open for 9% -> 12% of each run, Pallas kernels for 0% -> 0%
where the time goes in v1:
time: 216 us; the launch traced here: 214 us
  matrix products  58.4 us (27%)
  starting transfers between devices  55.1 us (26%)
  waiting for transfers between devices  47.9 us (22%)
  local copies, waits for them, and re-layouts  29 us (13%)
  other arithmetic  22.5 us (10%)
    ppermute x4, starting transfers between devices, shifted(): return lax.ppermute(value, axis, pairs)  17.1 us
    unnamed x26, local copies, waits for them, and re-layouts  16.4 us
    dot_general x4, matrix products, one_block(): jnp.einsum('qk,kd->qd', weight_bf, value_block, preferred_element_type=jn...  15.7 us
    dot_general x4, matrix products, key_terms(): jnp.einsum('qk,qd->kd', weight_bf, grad_rows, preferred_element_type=jnp....  10.9 us
    dot_general x4, matrix products, one_block(): jnp.einsum('qd,kd->qk', query_rows, key_block, preferred_element_type=jnp...  9.35 us
    dot_general x4, matrix products, score_grads(): jnp.einsum('qd,kd->qk', grad_rows, value_block, preferred_element_type=jn...  9.2 us
    all_to_all x1, waiting for transfers between devices, shards(): lax.all_to_all(query_in, 'head', split_axis=1, concat_axis=0, tiled=True)  8.55 us
    all_to_all x1, waiting for transfers between devices, shards(): lax.all_to_all(key_in, 'head', split_axis=1, concat_axis=0, tiled=True)  8.54 us
  transfers between devices with their start and end apart: 12, of which 7 were waited for; matrix products, arithmetic and copies ran while one was open for 12% of the time, Pallas kernels for 0%

profile of v1, /device:TPU:225, one launch (start us, length us, event | category | flops | bytes accessed | tf_op | source)
XLA Modules:
  0.0 214.4 jit_solution(13711695960462773591)
XLA Ops:
  2.6 6.8 %all-to-all-start.1 = ((bf16[128,16,128]{2,0,1:T(8,128)(2,1)}), bf16[128,16,128]{2,0,1:T(8,128)(2,1)S(1)}, u32[]{:S(2)}, u32[]{:S(2)}) async-start(bf16[128,16,128]{2,0,1:T(8,128)(2,1)} %copy_bitcast_fusion.1), calls=%async_computation.1 | async-start | bytes 1048576 | tf_op jit(solution)/shard_map/all_to_all | solution.py:67
  9.4 2.0 copy_bitcast_fusion
  11.3 8.5 %all-to-all-done.1 = bf16[128,16,128]{2,0,1:T(8,128)(2,1)S(1)} async-done(((bf16[128,16,128]{2,0,1:T(8,128)(2,1)}), bf16[128,16,128]{2,0,1:T(8,128)(2,1)S(1)}, u32[]{:S(2)}, u32[]{:S(2)}) %all-to-all-start.1) | async-done | bytes 524320 | tf_op jit(solution)/shard_map/all_to_all | solution.py:67
  19.9 3.6 %all-to-all-start.2 = ((bf16[128,16,128]{2,0,1:T(8,128)(2,1)}), bf16[128,16,128]{2,0,1:T(8,128)(2,1)S(1)}, u32[]{:S(2)}, u32[]{:S(2)}) async-start(bf16[128,16,128]{2,0,1:T(8,128)(2,1)} %copy_bitcast_fusion), calls=%async_computation.2 | async-start | bytes 1048576 | tf_op jit(solution)/shard_map/all_to_all | solution.py:68
  23.5 2.0 copy.70
  25.5 7.6 %all-to-all-done.2 = bf16[128,16,128]{2,0,1:T(8,128)(2,1)S(1)} async-done(((bf16[128,16,128]{2,0,1:T(8,128)(2,1)}), bf16[128,16,128]{2,0,1:T(8,128)(2,1)S(1)}, u32[]{:S(2)}, u32[]{:S(2)}) %all-to-all-start.2) | async-done | bytes 524320 | tf_op jit(solution)/shard_map/all_to_all | solution.py:68
  33.1 3.6 %all-to-all-start.3 = ((bf16[128,16,128]{0,2,1:T(8,128)(2,1)}), bf16[128,16,128]{0,2,1:T(8,128)(2,1)S(1)}, u32[]{:S(2)}, u32[]{:S(2)}) async-start(bf16[128,16,128]{0,2,1:T(8,128)(2,1)} %bitcast.18), calls=%async_computation.3 | async-start | bytes 1048576 | tf_op jit(solution)/shard_map/all_to_all | solution.py:69
  38.2 7.5 %collective-permute-start = (bf16[256,128]{1,0:T(8,128)(2,1)S(1)}, bf16[256,128]{1,0:T(8,128)(2,1)S(1)}, u32[]{:S(2)}, u32[]{:S(2)}) collective-permute-start(bf16[256,128]{1,0:T(8,128)(2,1)S(1)} %bitcast.150), channel_id=1, source_target_pairs={{0,16},{16,32},{32,48},{48,64},{64,80},{80,96},{96,112},{112,128},... | collective-permute-start | bytes 196616 | tf_op jit(solution)/shard_map/ppermute | solution.py:14
  45.7 1.9 collective-permute-start.1
  47.7 6.9 %all-to-all-start = ((bf16[128,16,128]{2,0,1:T(8,128)(2,1)}), bf16[128,16,128]{2,0,1:T(8,128)(2,1)S(1)}, u32[]{:S(2)}, u32[]{:S(2)}) async-start(bf16[128,16,128]{2,0,1:T(8,128)(2,1)} %copy_bitcast_fusion.2), calls=%async_computation | async-start | bytes 1048576 | tf_op jit(solution)/shard_map/all_to_all | solution.py:66
  56.6 8.5 %all-to-all-done = bf16[128,16,128]{2,0,1:T(8,128)(2,1)S(1)} async-done(((bf16[128,16,128]{2,0,1:T(8,128)(2,1)}), bf16[128,16,128]{2,0,1:T(8,128)(2,1)S(1)}, u32[]{:S(2)}, u32[]{:S(2)}) %all-to-all-start) | async-done | bytes 524320 | tf_op jit(solution)/shard_map/all_to_all | solution.py:66
  65.1 79.0 %while.33 = (s32[]{:T(128)}, bf16[4,512,128]{2,1,0:T(8,128)(2,1)}, bf16[4,512,128]{2,1,0:T(8,128)(2,1)}, f32[4,2304,128]{2,1,0:T(8,128)}, f32[4,2304,128]{2,1,0:...) while((s32[]{:T(128)}, bf16[4,512,128]{2,1,0:T(8,128)(2,1)}, ...), condition=%wide.region_8.9_spmd, body=%wide.region_2.8_spmd.sunk | while | flops 1855588608 | bytes 75382872 | solution.py:107
  67.0 2.3 %select_reduce_fusion.4 = (f32[512]{0:T(512)S(1)}, f32[512,2304]{1,0:T(8,128)S(1)}) fusion(s32[512]{0:T(512)S(1)} %bitcast.144, s32[2304]{0:T(1024)S(1)} %get-tuple-element.461, s32[2304]{0:T(1024)S(1)} %compare_select_fusion.4, s32[512]{0:T(512)S(1)} %compare_select_fusion.5, bf16[2304,128]{1,0:T(8,128)(2,1)} %get-tuple-element.463, ...), kind=kOutput, calls=%fused_computation.6.clone.1 | convolution fusion | flops 309067264 | bytes 5470212 | tf_op jit(solution)/shard_map/while/body/eval_jaxpr/while/body/eval_jaxpr/qd,kd->qk/dot_general | solution.py:44
  69.4 1.7 select_reduce_fusion.5
  71.6 2.7 %fusion.56 = f32[4,2304,128]{2,1,0:T(8,128)} fusion(f32[4,2304,128]{2,1,0:T(8,128)} %get-tuple-element.443, s32[]{:T(128)} %get-tuple-element.439, bf16[1,512,128]{2,1,0:T(8,128)(2,1)S(1)} %constant_dynamic-slice_fusion.4, f32[512,2304]{1,0:T(8,128)S(1)} %get-tuple-element.421, f32[512]{0:T(512)S(1)} %log_add_fusion.2, ...), kind=kOutput, calls=%fused_computation.11.clone.1 | convolution fusion | flops 309067776 | bytes 6054400 | tf_op jit(solution)/shard_map/while/body/eval_jaxpr/while/body/eval_jaxpr/qk,qd->kd/dot_general | solution.py:38
  74.5 3.9 %multiply_reduce_fusion.2 = (f32[512]{0:T(512)S(1)}, bf16[512,128]{0,1:T(8,128)(2,1)S(1)}) fusion(bf16[1,512,128]{1,2,0:T(8,128)(2,1)S(1)} %copy.95, bf16[2304,128]{1,0:T(8,128)(2,1)S(1)} %copy-done.3, f32[512,2304]{1,0:T(8,128)} %copy-done.1, f32[512]{0:T(512)S(1)} %log_add_fusion.2, s32[512]{0:T(512)S(1)} %bitcast.147, ...), kind=kOutput, calls=%fused_computation.20.clone.1 | convolution fusion | flops 309394944 | bytes 5597184 | tf_op jit(solution)/shard_map/while/body/eval_jaxpr/while/body/eval_jaxpr/qk,kd->qd/dot_general | solution.py:52
  78.4 2.3 %fusion.53 = bf16[512,2304]{1,0:T(8,128)(2,1)S(1)} fusion(bf16[2304,128]{1,0:T(8,128)(2,1)S(1)} %copy-done.3, f32[512,2304]{1,0:T(8,128)S(1)} %bitcast.121, f32[512]{0:T(512)S(1)} %get-tuple-element.424, f32[512]{0:T(512)S(1)} %log_add_fusion.2, bf16[1,512,128]{2,1,0:T(8,128)(2,1)S(1)} %constant_dynamic-slice_fusion.4, s32[512]{0:T(512)S(1)} %bitcast.148, ...), kind=kOutput, calls=%fused_computation.9.clone.1 | convolution fusion | flops 312606720 | bytes 7825408 | tf_op jit(solution)/shard_map/while/body/eval_jaxpr/while/body/eval_jaxpr/qd,kd->qk/dot_general | solution.py:32
  80.8 1.8 fusion.55
  86.8 2.3 %select_reduce_fusion.4 = (f32[512]{0:T(512)S(1)}, f32[512,2304]{1,0:T(8,128)S(1)}) fusion(s32[512]{0:T(512)S(1)} %bitcast.144, s32[2304]{0:T(1024)S(1)} %get-tuple-element.461, s32[2304]{0:T(1024)S(1)} %compare_select_fusion.4, s32[512]{0:T(512)S(1)} %compare_select_fusion.5, bf16[2304,128]{1,0:T(8,128)(2,1)} %get-tuple-element.463, ...), kind=kOutput, calls=%fused_computation.6.clone.1 | convolution fusion | flops 309067264 | bytes 5470212 | tf_op jit(solution)/shard_map/while/body/eval_jaxpr/while/body/eval_jaxpr/qd,kd->qk/dot_general | solution.py:44
  89.1 1.7 select_reduce_fusion.5
  91.3 2.7 %fusion.56 = f32[4,2304,128]{2,1,0:T(8,128)} fusion(f32[4,2304,128]{2,1,0:T(8,128)} %get-tuple-element.443, s32[]{:T(128)} %get-tuple-element.439, bf16[1,512,128]{2,1,0:T(8,128)(2,1)S(1)} %constant_dynamic-slice_fusion.4, f32[512,2304]{1,0:T(8,128)S(1)} %get-tuple-element.421, f32[512]{0:T(512)S(1)} %log_add_fusion.2, ...), kind=kOutput, calls=%fused_computation.11.clone.1 | convolution fusion | flops 309067776 | bytes 6054400 | tf_op jit(solution)/shard_map/while/body/eval_jaxpr/while/body/eval_jaxpr/qk,qd->kd/dot_general | solution.py:38
  94.2 3.9 %multiply_reduce_fusion.2 = (f32[512]{0:T(512)S(1)}, bf16[512,128]{0,1:T(8,128)(2,1)S(1)}) fusion(bf16[1,512,128]{1,2,0:T(8,128)(2,1)S(1)} %copy.95, bf16[2304,128]{1,0:T(8,128)(2,1)S(1)} %copy-done.3, f32[512,2304]{1,0:T(8,128)} %copy-done.1, f32[512]{0:T(512)S(1)} %log_add_fusion.2, s32[512]{0:T(512)S(1)} %bitcast.147, ...), kind=kOutput, calls=%fused_computation.20.clone.1 | convolution fusion | flops 309394944 | bytes 5597184 | tf_op jit(solution)/shard_map/while/body/eval_jaxpr/while/body/eval_jaxpr/qk,kd->qd/dot_general | solution.py:52
  98.2 2.3 %fusion.53 = bf16[512,2304]{1,0:T(8,128)(2,1)S(1)} fusion(bf16[2304,128]{1,0:T(8,128)(2,1)S(1)} %copy-done.3, f32[512,2304]{1,0:T(8,128)S(1)} %bitcast.121, f32[512]{0:T(512)S(1)} %get-tuple-element.424, f32[512]{0:T(512)S(1)} %log_add_fusion.2, bf16[1,512,128]{2,1,0:T(8,128)(2,1)S(1)} %constant_dynamic-slice_fusion.4, s32[512]{0:T(512)S(1)} %bitcast.148, ...), kind=kOutput, calls=%fused_computation.9.clone.1 | convolution fusion | flops 312606720 | bytes 7825408 | tf_op jit(solution)/shard_map/while/body/eval_jaxpr/while/body/eval_jaxpr/qd,kd->qk/dot_general | solution.py:32
  100.5 1.9 fusion.55
  106.5 2.3 %select_reduce_fusion.4 = (f32[512]{0:T(512)S(1)}, f32[512,2304]{1,0:T(8,128)S(1)}) fusion(s32[512]{0:T(512)S(1)} %bitcast.144, s32[2304]{0:T(1024)S(1)} %get-tuple-element.461, s32[2304]{0:T(1024)S(1)} %compare_select_fusion.4, s32[512]{0:T(512)S(1)} %compare_select_fusion.5, bf16[2304,128]{1,0:T(8,128)(2,1)} %get-tuple-element.463, ...), kind=kOutput, calls=%fused_computation.6.clone.1 | convolution fusion | flops 309067264 | bytes 5470212 | tf_op jit(solution)/shard_map/while/body/eval_jaxpr/while/body/eval_jaxpr/qd,kd->qk/dot_general | solution.py:44
  108.9 1.7 select_reduce_fusion.5
  111.1 2.7 %fusion.56 = f32[4,2304,128]{2,1,0:T(8,128)} fusion(f32[4,2304,128]{2,1,0:T(8,128)} %get-tuple-element.443, s32[]{:T(128)} %get-tuple-element.439, bf16[1,512,128]{2,1,0:T(8,128)(2,1)S(1)} %constant_dynamic-slice_fusion.4, f32[512,2304]{1,0:T(8,128)S(1)} %get-tuple-element.421, f32[512]{0:T(512)S(1)} %log_add_fusion.2, ...), kind=kOutput, calls=%fused_computation.11.clone.1 | convolution fusion | flops 309067776 | bytes 6054400 | tf_op jit(solution)/shard_map/while/body/eval_jaxpr/while/body/eval_jaxpr/qk,qd->kd/dot_general | solution.py:38
  113.9 3.9 %multiply_reduce_fusion.2 = (f32[512]{0:T(512)S(1)}, bf16[512,128]{0,1:T(8,128)(2,1)S(1)}) fusion(bf16[1,512,128]{1,2,0:T(8,128)(2,1)S(1)} %copy.95, bf16[2304,128]{1,0:T(8,128)(2,1)S(1)} %copy-done.3, f32[512,2304]{1,0:T(8,128)} %copy-done.1, f32[512]{0:T(512)S(1)} %log_add_fusion.2, s32[512]{0:T(512)S(1)} %bitcast.147, ...), kind=kOutput, calls=%fused_computation.20.clone.1 | convolution fusion | flops 309394944 | bytes 5597184 | tf_op jit(solution)/shard_map/while/body/eval_jaxpr/while/body/eval_jaxpr/qk,kd->qd/dot_general | solution.py:52
  117.9 2.3 %fusion.53 = bf16[512,2304]{1,0:T(8,128)(2,1)S(1)} fusion(bf16[2304,128]{1,0:T(8,128)(2,1)S(1)} %copy-done.3, f32[512,2304]{1,0:T(8,128)S(1)} %bitcast.121, f32[512]{0:T(512)S(1)} %get-tuple-element.424, f32[512]{0:T(512)S(1)} %log_add_fusion.2, bf16[1,512,128]{2,1,0:T(8,128)(2,1)S(1)} %constant_dynamic-slice_fusion.4, s32[512]{0:T(512)S(1)} %bitcast.148, ...), kind=kOutput, calls=%fused_computation.9.clone.1 | convolution fusion | flops 312606720 | bytes 7825408 | tf_op jit(solution)/shard_map/while/body/eval_jaxpr/while/body/eval_jaxpr/qd,kd->qk/dot_general | solution.py:32
  120.2 1.9 fusion.55
  126.2 2.3 %select_reduce_fusion.4 = (f32[512]{0:T(512)S(1)}, f32[512,2304]{1,0:T(8,128)S(1)}) fusion(s32[512]{0:T(512)S(1)} %bitcast.144, s32[2304]{0:T(1024)S(1)} %get-tuple-element.461, s32[2304]{0:T(1024)S(1)} %compare_select_fusion.4, s32[512]{0:T(512)S(1)} %compare_select_fusion.5, bf16[2304,128]{1,0:T(8,128)(2,1)} %get-tuple-element.463, ...), kind=kOutput, calls=%fused_computation.6.clone.1 | convolution fusion | flops 309067264 | bytes 5470212 | tf_op jit(solution)/shard_map/while/body/eval_jaxpr/while/body/eval_jaxpr/qd,kd->qk/dot_general | solution.py:44
  128.6 1.7 select_reduce_fusion.5
  130.8 2.8 %fusion.56 = f32[4,2304,128]{2,1,0:T(8,128)} fusion(f32[4,2304,128]{2,1,0:T(8,128)} %get-tuple-element.443, s32[]{:T(128)} %get-tuple-element.439, bf16[1,512,128]{2,1,0:T(8,128)(2,1)S(1)} %constant_dynamic-slice_fusion.4, f32[512,2304]{1,0:T(8,128)S(1)} %get-tuple-element.421, f32[512]{0:T(512)S(1)} %log_add_fusion.2, ...), kind=kOutput, calls=%fused_computation.11.clone.1 | convolution fusion | flops 309067776 | bytes 6054400 | tf_op jit(solution)/shard_map/while/body/eval_jaxpr/while/body/eval_jaxpr/qk,qd->kd/dot_general | solution.py:38
  133.7 3.9 %multiply_reduce_fusion.2 = (f32[512]{0:T(512)S(1)}, bf16[512,128]{0,1:T(8,128)(2,1)S(1)}) fusion(bf16[1,512,128]{1,2,0:T(8,128)(2,1)S(1)} %copy.95, bf16[2304,128]{1,0:T(8,128)(2,1)S(1)} %copy-done.3, f32[512,2304]{1,0:T(8,128)} %copy-done.1, f32[512]{0:T(512)S(1)} %log_add_fusion.2, s32[512]{0:T(512)S(1)} %bitcast.147, ...), kind=kOutput, calls=%fused_computation.20.clone.1 | convolution fusion | flops 309394944 | bytes 5597184 | tf_op jit(solution)/shard_map/while/body/eval_jaxpr/while/body/eval_jaxpr/qk,kd->qd/dot_general | solution.py:52
  137.7 2.3 %fusion.53 = bf16[512,2304]{1,0:T(8,128)(2,1)S(1)} fusion(bf16[2304,128]{1,0:T(8,128)(2,1)S(1)} %copy-done.3, f32[512,2304]{1,0:T(8,128)S(1)} %bitcast.121, f32[512]{0:T(512)S(1)} %get-tuple-element.424, f32[512]{0:T(512)S(1)} %log_add_fusion.2, bf16[1,512,128]{2,1,0:T(8,128)(2,1)S(1)} %constant_dynamic-slice_fusion.4, s32[512]{0:T(512)S(1)} %bitcast.148, ...), kind=kOutput, calls=%fused_computation.9.clone.1 | convolution fusion | flops 312606720 | bytes 7825408 | tf_op jit(solution)/shard_map/while/body/eval_jaxpr/while/body/eval_jaxpr/qd,kd->qk/dot_general | solution.py:32
  140.0 1.9 fusion.55
  144.2 2.7 %reduce_sum.64 = f32[2304,128]{1,0:T(8,128)S(1)} reduce(f32[4,2304,128]{2,1,0:T(8,128)} %get-tuple-element.212, f32[]{:T(128)} %constant.129.clone.1), dimensions={0}, to_apply=%region_9.10 | reduce | flops 884736 | bytes 5898244 | tf_op jit(solution)/shard_map/while/body/eval_jaxpr/reduce_sum | solution.py:113
  146.9 3.8 %collective-permute-start.2 = (f32[1,256,128]{2,1,0:T(8,128)S(1)}, f32[1,256,128]{2,1,0:T(8,128)S(1)}, u32[]{:S(2)}, u32[]{:S(2)}) collective-permute-start(f32[1,256,128]{2,1,0:T(8,128)S(1)} %slice.116), channel_id=1, source_target_pairs={{16,0},{32,16},{48,32},{64,48},{80,64},{96,80},{112,96},{128,112},... | collective-permute-start | bytes 393224 | tf_op jit(solution)/shard_map/ppermute | solution.py:14
  150.8 3.6 %all-to-all-start.4 = ((bf16[16,128,128]{2,1,0:T(8,128)(2,1)}), bf16[16,128,128]{2,1,0:T(8,128)(2,1)S(1)}, u32[]{:S(2)}, u32[]{:S(2)}) async-start(bf16[16,128,128]{2,1,0:T(8,128)(2,1)} %bitcast.21), calls=%async_computation.4 | async-start | bytes 1048576 | tf_op jit(solution)/shard_map/all_to_all | solution.py:123
  162.5 3.3 %all-to-all-done.4 = bf16[16,128,128]{2,1,0:T(8,128)(2,1)S(1)} async-done(((bf16[16,128,128]{2,1,0:T(8,128)(2,1)}), bf16[16,128,128]{2,1,0:T(8,128)(2,1)S(1)}, u32[]{:S(2)}, u32[]{:S(2)}) %all-to-all-start.4) | async-done | bytes 524320 | tf_op jit(solution)/shard_map/all_to_all | solution.py:123
  165.7 3.8 %all-to-all-start.5 = ((bf16[16,128,128]{2,1,0:T(8,128)(2,1)}), bf16[16,128,128]{2,1,0:T(8,128)(2,1)S(1)}, u32[]{:S(2)}, u32[]{:S(2)}) async-start(bf16[16,128,128]{2,1,0:T(8,128)(2,1)} %bitcast.149), calls=%async_computation.5 | async-start | bytes 1048576 | tf_op jit(solution)/shard_map/all_to_all | solution.py:144
  171.4 8.4 %all-to-all-done.5 = bf16[16,128,128]{2,1,0:T(8,128)(2,1)S(1)} async-done(((bf16[16,128,128]{2,1,0:T(8,128)(2,1)}), bf16[16,128,128]{2,1,0:T(8,128)(2,1)S(1)}, u32[]{:S(2)}, u32[]{:S(2)}) %all-to-all-start.5) | async-done | bytes 524320 | tf_op jit(solution)/shard_map/all_to_all | solution.py:144
  179.8 3.6 %all-to-all-start.6 = ((bf16[16,128,128]{2,1,0:T(8,128)(2,1)}), bf16[16,128,128]{2,1,0:T(8,128)(2,1)S(1)}, u32[]{:S(2)}, u32[]{:S(2)}) async-start(bf16[16,128,128]{2,1,0:T(8,128)(2,1)} %constant_dynamic-update-slice_fusion.1), calls=%async_computation.6 | async-start | bytes 1048576 | tf_op jit(solution)/shard_map/all_to_all | solution.py:133
  183.4 2.7 %reduce_sum.65 = f32[2304,128]{1,0:T(8,128)S(1)} reduce(f32[4,2304,128]{2,1,0:T(8,128)} %get-tuple-element.213, f32[]{:T(128)} %constant.129.clone.1), dimensions={0}, to_apply=%region_10.11 | reduce | flops 884736 | bytes 5898244 | tf_op jit(solution)/shard_map/while/body/eval_jaxpr/reduce_sum | solution.py:114
  186.1 3.9 %collective-permute-start.3 = (f32[1,256,128]{2,1,0:T(8,128)S(1)}, f32[1,256,128]{2,1,0:T(8,128)S(1)}, u32[]{:S(2)}, u32[]{:S(2)}) collective-permute-start(f32[1,256,128]{2,1,0:T(8,128)S(1)} %slice.119), channel_id=1, source_target_pairs={{16,0},{32,16},{48,32},{64,48},{80,64},{96,80},{112,96},{128,112},... | collective-permute-start | bytes 393224 | tf_op jit(solution)/shard_map/ppermute | solution.py:14
  190.9 3.1 %collective-permute-done.3 = f32[1,256,128]{2,1,0:T(8,128)S(1)} collective-permute-done((f32[1,256,128]{2,1,0:T(8,128)S(1)}, f32[1,256,128]{2,1,0:T(8,128)S(1)}, u32[]{:S(2)}, u32[]{:S(2)}) %collective-permute-start.3) | collective-permute-done | bytes 131104 | tf_op jit(solution)/shard_map/ppermute | solution.py:14
  194.6 6.3 %all-to-all-start.7 = ((bf16[16,128,128]{2,1,0:T(8,128)(2,1)}), bf16[16,128,128]{2,1,0:T(8,128)(2,1)S(1)}, u32[]{:S(2)}, u32[]{:S(2)}) async-start(bf16[16,128,128]{2,1,0:T(8,128)(2,1)} %bitcast.31), calls=%async_computation.7 | async-start | bytes 1048576 | tf_op jit(solution)/shard_map/all_to_all | solution.py:146
  204.8 8.4 %all-to-all-done.7 = bf16[16,128,128]{2,1,0:T(8,128)(2,1)S(1)} async-done(((bf16[16,128,128]{2,1,0:T(8,128)(2,1)}), bf16[16,128,128]{2,1,0:T(8,128)(2,1)S(1)}, u32[]{:S(2)}, u32[]{:S(2)}) %all-to-all-start.7) | async-done | bytes 524320 | tf_op jit(solution)/shard_map/all_to_all | solution.py:146
  (188 shorter events, 41.0 us)
Async XLA Ops:
  0.6 36.1 %copy-start.7 = (s32[512]{0:T(512)S(1)}, s32[512]{0:T(512)}, u32[]{:S(2)}) copy-start(s32[512]{0:T(512)} %param.15) | copy-start | bytes 6148
  1.7 35.6 %copy-start.4 = (bf16[128,2048]{1,0:T(8,128)(2,1)S(1)}, bf16[128,2048]{1,0:T(8,128)(2,1)}, u32[]{:S(2)}) copy-start(bf16[128,2048]{1,0:T(8,128)(2,1)} %param.11) | copy-start | bytes 1572868
  2.6 17.3 %all-to-all-start.1 = ((bf16[128,16,128]{2,0,1:T(8,128)(2,1)}), bf16[128,16,128]{2,0,1:T(8,128)(2,1)S(1)}, u32[]{:S(2)}, u32[]{:S(2)}) async-start(bf16[128,16,128]{2,0,1:T(8,128)(2,1)} %copy_bitcast_fusion.1), calls=%async_computation.1 | async-start | bytes 1048576 | tf_op jit(solution)/shard_map/all_to_all | solution.py:67
  19.9 13.2 %all-to-all-start.2 = ((bf16[128,16,128]{2,0,1:T(8,128)(2,1)}), bf16[128,16,128]{2,0,1:T(8,128)(2,1)S(1)}, u32[]{:S(2)}, u32[]{:S(2)}) async-start(bf16[128,16,128]{2,0,1:T(8,128)(2,1)} %copy_bitcast_fusion), calls=%async_computation.2 | async-start | bytes 1048576 | tf_op jit(solution)/shard_map/all_to_all | solution.py:68
  33.1 14.5 %all-to-all-start.3 = ((bf16[128,16,128]{0,2,1:T(8,128)(2,1)}), bf16[128,16,128]{0,2,1:T(8,128)(2,1)S(1)}, u32[]{:S(2)}, u32[]{:S(2)}) async-start(bf16[128,16,128]{0,2,1:T(8,128)(2,1)} %bitcast.18), calls=%async_computation.3 | async-start | bytes 1048576 | tf_op jit(solution)/shard_map/all_to_all | solution.py:69
  38.2 16.6 %collective-permute-start = (bf16[256,128]{1,0:T(8,128)(2,1)S(1)}, bf16[256,128]{1,0:T(8,128)(2,1)S(1)}, u32[]{:S(2)}, u32[]{:S(2)}) collective-permute-start(bf16[256,128]{1,0:T(8,128)(2,1)S(1)} %bitcast.150), channel_id=1, source_target_pairs={{0,16},{16,32},{32,48},{48,64},{64,80},{80,96},{96,112},{112,128},... | collective-permute-start | bytes 196616 | tf_op jit(solution)/shard_map/ppermute | solution.py:14
  45.7 10.0 %collective-permute-start.1 = (bf16[256,128]{1,0:T(8,128)(2,1)S(1)}, bf16[256,128]{1,0:T(8,128)(2,1)S(1)}, u32[]{:S(2)}, u32[]{:S(2)}) collective-permute-start(bf16[256,128]{1,0:T(8,128)(2,1)S(1)} %bitcast.151), channel_id=1, source_target_pairs={{0,16},{16,32},{32,48},{48,64},{64,80},{80,96},{96,112},{112,128},... | collective-permute-start | bytes 196616 | tf_op jit(solution)/shard_map/ppermute | solution.py:14
  47.7 17.5 %all-to-all-start = ((bf16[128,16,128]{2,0,1:T(8,128)(2,1)}), bf16[128,16,128]{2,0,1:T(8,128)(2,1)S(1)}, u32[]{:S(2)}, u32[]{:S(2)}) async-start(bf16[128,16,128]{2,0,1:T(8,128)(2,1)} %copy_bitcast_fusion.2), calls=%async_computation | async-start | bytes 1048576 | tf_op jit(solution)/shard_map/all_to_all | solution.py:66
  65.1 6.0 %copy-start.5 = (s32[4,512]{1,0:T(4,128)}, s32[4,512]{1,0:T(4,128)S(1)}, u32[]{:S(2)}) copy-start(s32[4,512]{1,0:T(4,128)S(1)} %get-tuple-element.458) | copy-start | bytes 24580 | tf_op jit(solution)/shard_map/while/body/eval_jaxpr/while
  65.1 6.0 %copy-start.8 = (s32[5,1]{0,1:T(1,128)}, s32[5,1]{0,1:T(1,128)S(1)}, u32[]{:S(2)}) copy-start(s32[5,1]{0,1:T(1,128)S(1)} %get-tuple-element.459) | copy-start | bytes 64 | tf_op jit(solution)/shard_map/while/body/eval_jaxpr/while
  69.4 2.2 %copy-start.1 = (f32[512,2304]{1,0:T(8,128)}, f32[512,2304]{1,0:T(8,128)S(1)}, u32[]{:S(2)}) copy-start(f32[512,2304]{1,0:T(8,128)S(1)} %get-tuple-element.421) | copy-start | bytes 14155780 | tf_op jit(solution)/shard_map/while/body/eval_jaxpr/while
  71.6 2.9 %copy-start.3 = (bf16[2304,128]{1,0:T(8,128)(2,1)S(1)}, bf16[2304,128]{1,0:T(8,128)(2,1)}, u32[]{:S(2)}) copy-start(bf16[2304,128]{1,0:T(8,128)(2,1)} %get-tuple-element.464) | copy-start | bytes 1769476 | tf_op jit(solution)/shard_map/while/body/eval_jaxpr/while
  74.4 4.0 %slice-start = ((s8[4718592]{0:T(1024)(128)(4,1)}), s8[4194304]{0:T(1024)(128)(4,1)S(1)}, s32[]{:S(2)}) async-start(s8[4718592]{0:T(1024)(128)(4,1)} %bitcast.120), calls=%async_computation.8 | async-start | bytes 8388608 | tf_op jit(solution)/shard_map/while/body/eval_jaxpr/while
  74.5 4.0 %slice-start.1 = ((s8[4718592]{0:T(1024)(128)(4,1)}), s8[524288]{0:T(1024)(128)(4,1)S(1)}, s32[]{:S(2)}) async-start(s8[4718592]{0:T(1024)(128)(4,1)} %bitcast.120), calls=%async_computation.9 | async-start | bytes 1048576 | tf_op jit(solution)/shard_map/while/body/eval_jaxpr/while
  80.7 4.1 %copy-start.6 = (s32[4,512]{1,0:T(4,128)S(1)}, s32[4,512]{1,0:T(4,128)}, u32[]{:S(2)}) copy-start(s32[4,512]{1,0:T(4,128)} %copy-done.5) | copy-start | bytes 24580 | tf_op jit(solution)/shard_map/while/body/eval_jaxpr/while
  80.8 4.1 %copy-start.9 = (s32[5,1]{0,1:T(1,128)S(1)}, s32[5,1]{0,1:T(1,128)}, u32[]{:S(2)}) copy-start(s32[5,1]{0,1:T(1,128)} %copy-done.8) | copy-start | bytes 64 | tf_op jit(solution)/shard_map/while/body/eval_jaxpr/while
  84.9 6.0 %copy-start.5 = (s32[4,512]{1,0:T(4,128)}, s32[4,512]{1,0:T(4,128)S(1)}, u32[]{:S(2)}) copy-start(s32[4,512]{1,0:T(4,128)S(1)} %get-tuple-element.458) | copy-start | bytes 24580 | tf_op jit(solution)/shard_map/while/body/eval_jaxpr/while
  84.9 6.0 %copy-start.8 = (s32[5,1]{0,1:T(1,128)}, s32[5,1]{0,1:T(1,128)S(1)}, u32[]{:S(2)}) copy-start(s32[5,1]{0,1:T(1,128)S(1)} %get-tuple-element.459) | copy-start | bytes 64 | tf_op jit(solution)/shard_map/while/body/eval_jaxpr/while
  89.1 2.2 %copy-start.1 = (f32[512,2304]{1,0:T(8,128)}, f32[512,2304]{1,0:T(8,128)S(1)}, u32[]{:S(2)}) copy-start(f32[512,2304]{1,0:T(8,128)S(1)} %get-tuple-element.421) | copy-start | bytes 14155780 | tf_op jit(solution)/shard_map/while/body/eval_jaxpr/while
  91.3 2.8 %copy-start.3 = (bf16[2304,128]{1,0:T(8,128)(2,1)S(1)}, bf16[2304,128]{1,0:T(8,128)(2,1)}, u32[]{:S(2)}) copy-start(bf16[2304,128]{1,0:T(8,128)(2,1)} %get-tuple-element.464) | copy-start | bytes 1769476 | tf_op jit(solution)/shard_map/while/body/eval_jaxpr/while
  94.2 4.0 %slice-start = ((s8[4718592]{0:T(1024)(128)(4,1)}), s8[4194304]{0:T(1024)(128)(4,1)S(1)}, s32[]{:S(2)}) async-start(s8[4718592]{0:T(1024)(128)(4,1)} %bitcast.120), calls=%async_computation.8 | async-start | bytes 8388608 | tf_op jit(solution)/shard_map/while/body/eval_jaxpr/while
  94.2 4.0 %slice-start.1 = ((s8[4718592]{0:T(1024)(128)(4,1)}), s8[524288]{0:T(1024)(128)(4,1)S(1)}, s32[]{:S(2)}) async-start(s8[4718592]{0:T(1024)(128)(4,1)} %bitcast.120), calls=%async_computation.9 | async-start | bytes 1048576 | tf_op jit(solution)/shard_map/while/body/eval_jaxpr/while
  100.5 4.1 %copy-start.6 = (s32[4,512]{1,0:T(4,128)S(1)}, s32[4,512]{1,0:T(4,128)}, u32[]{:S(2)}) copy-start(s32[4,512]{1,0:T(4,128)} %copy-done.5) | copy-start | bytes 24580 | tf_op jit(solution)/shard_map/while/body/eval_jaxpr/while
  100.5 4.1 %copy-start.9 = (s32[5,1]{0,1:T(1,128)S(1)}, s32[5,1]{0,1:T(1,128)}, u32[]{:S(2)}) copy-start(s32[5,1]{0,1:T(1,128)} %copy-done.8) | copy-start | bytes 64 | tf_op jit(solution)/shard_map/while/body/eval_jaxpr/while
  104.6 6.0 %copy-start.5 = (s32[4,512]{1,0:T(4,128)}, s32[4,512]{1,0:T(4,128)S(1)}, u32[]{:S(2)}) copy-start(s32[4,512]{1,0:T(4,128)S(1)} %get-tuple-element.458) | copy-start | bytes 24580 | tf_op jit(solution)/shard_map/while/body/eval_jaxpr/while
  104.6 6.0 %copy-start.8 = (s32[5,1]{0,1:T(1,128)}, s32[5,1]{0,1:T(1,128)S(1)}, u32[]{:S(2)}) copy-start(s32[5,1]{0,1:T(1,128)S(1)} %get-tuple-element.459) | copy-start | bytes 64 | tf_op jit(solution)/shard_map/while/body/eval_jaxpr/while
  108.9 2.2 %copy-start.1 = (f32[512,2304]{1,0:T(8,128)}, f32[512,2304]{1,0:T(8,128)S(1)}, u32[]{:S(2)}) copy-start(f32[512,2304]{1,0:T(8,128)S(1)} %get-tuple-element.421) | copy-start | bytes 14155780 | tf_op jit(solution)/shard_map/while/body/eval_jaxpr/while
  111.1 2.8 %copy-start.3 = (bf16[2304,128]{1,0:T(8,128)(2,1)S(1)}, bf16[2304,128]{1,0:T(8,128)(2,1)}, u32[]{:S(2)}) copy-start(bf16[2304,128]{1,0:T(8,128)(2,1)} %get-tuple-element.464) | copy-start | bytes 1769476 | tf_op jit(solution)/shard_map/while/body/eval_jaxpr/while
  113.9 4.0 %slice-start = ((s8[4718592]{0:T(1024)(128)(4,1)}), s8[4194304]{0:T(1024)(128)(4,1)S(1)}, s32[]{:S(2)}) async-start(s8[4718592]{0:T(1024)(128)(4,1)} %bitcast.120), calls=%async_computation.8 | async-start | bytes 8388608 | tf_op jit(solution)/shard_map/while/body/eval_jaxpr/while
  113.9 4.0 %slice-start.1 = ((s8[4718592]{0:T(1024)(128)(4,1)}), s8[524288]{0:T(1024)(128)(4,1)S(1)}, s32[]{:S(2)}) async-start(s8[4718592]{0:T(1024)(128)(4,1)} %bitcast.120), calls=%async_computation.9 | async-start | bytes 1048576 | tf_op jit(solution)/shard_map/while/body/eval_jaxpr/while
  120.2 1.9 copy-start.2
  120.2 4.1 %copy-start.6 = (s32[4,512]{1,0:T(4,128)S(1)}, s32[4,512]{1,0:T(4,128)}, u32[]{:S(2)}) copy-start(s32[4,512]{1,0:T(4,128)} %copy-done.5) | copy-start | bytes 24580 | tf_op jit(solution)/shard_map/while/body/eval_jaxpr/while
  120.2 4.1 %copy-start.9 = (s32[5,1]{0,1:T(1,128)S(1)}, s32[5,1]{0,1:T(1,128)}, u32[]{:S(2)}) copy-start(s32[5,1]{0,1:T(1,128)} %copy-done.8) | copy-start | bytes 64 | tf_op jit(solution)/shard_map/while/body/eval_jaxpr/while
  124.3 6.0 %copy-start.5 = (s32[4,512]{1,0:T(4,128)}, s32[4,512]{1,0:T(4,128)S(1)}, u32[]{:S(2)}) copy-start(s32[4,512]{1,0:T(4,128)S(1)} %get-tuple-element.458) | copy-start | bytes 24580 | tf_op jit(solution)/shard_map/while/body/eval_jaxpr/while
  124.3 6.0 %copy-start.8 = (s32[5,1]{0,1:T(1,128)}, s32[5,1]{0,1:T(1,128)S(1)}, u32[]{:S(2)}) copy-start(s32[5,1]{0,1:T(1,128)S(1)} %get-tuple-element.459) | copy-start | bytes 64 | tf_op jit(solution)/shard_map/while/body/eval_jaxpr/while
  128.6 2.2 %copy-start.1 = (f32[512,2304]{1,0:T(8,128)}, f32[512,2304]{1,0:T(8,128)S(1)}, u32[]{:S(2)}) copy-start(f32[512,2304]{1,0:T(8,128)S(1)} %get-tuple-element.421) | copy-start | bytes 14155780 | tf_op jit(solution)/shard_map/while/body/eval_jaxpr/while
  130.8 2.9 %copy-start.3 = (bf16[2304,128]{1,0:T(8,128)(2,1)S(1)}, bf16[2304,128]{1,0:T(8,128)(2,1)}, u32[]{:S(2)}) copy-start(bf16[2304,128]{1,0:T(8,128)(2,1)} %get-tuple-element.464) | copy-start | bytes 1769476 | tf_op jit(solution)/shard_map/while/body/eval_jaxpr/while
  133.7 4.0 %slice-start = ((s8[4718592]{0:T(1024)(128)(4,1)}), s8[4194304]{0:T(1024)(128)(4,1)S(1)}, s32[]{:S(2)}) async-start(s8[4718592]{0:T(1024)(128)(4,1)} %bitcast.120), calls=%async_computation.8 | async-start | bytes 8388608 | tf_op jit(solution)/shard_map/while/body/eval_jaxpr/while
  133.7 4.0 %slice-start.1 = ((s8[4718592]{0:T(1024)(128)(4,1)}), s8[524288]{0:T(1024)(128)(4,1)S(1)}, s32[]{:S(2)}) async-start(s8[4718592]{0:T(1024)(128)(4,1)} %bitcast.120), calls=%async_computation.9 | async-start | bytes 1048576 | tf_op jit(solution)/shard_map/while/body/eval_jaxpr/while
  140.0 1.9 copy-start.2
  140.0 4.1 %copy-start.6 = (s32[4,512]{1,0:T(4,128)S(1)}, s32[4,512]{1,0:T(4,128)}, u32[]{:S(2)}) copy-start(s32[4,512]{1,0:T(4,128)} %copy-done.5) | copy-start | bytes 24580 | tf_op jit(solution)/shard_map/while/body/eval_jaxpr/while
  140.0 4.1 %copy-start.9 = (s32[5,1]{0,1:T(1,128)S(1)}, s32[5,1]{0,1:T(1,128)}, u32[]{:S(2)}) copy-start(s32[5,1]{0,1:T(1,128)} %copy-done.8) | copy-start | bytes 64 | tf_op jit(solution)/shard_map/while/body/eval_jaxpr/while
  146.9 7.5 %collective-permute-start.2 = (f32[1,256,128]{2,1,0:T(8,128)S(1)}, f32[1,256,128]{2,1,0:T(8,128)S(1)}, u32[]{:S(2)}, u32[]{:S(2)}) collective-permute-start(f32[1,256,128]{2,1,0:T(8,128)S(1)} %slice.116), channel_id=1, source_target_pairs={{16,0},{32,16},{48,32},{64,48},{80,64},{96,80},{112,96},{128,112},... | collective-permute-start | bytes 393224 | tf_op jit(solution)/shard_map/ppermute | solution.py:14
  150.8 15.0 %all-to-all-start.4 = ((bf16[16,128,128]{2,1,0:T(8,128)(2,1)}), bf16[16,128,128]{2,1,0:T(8,128)(2,1)S(1)}, u32[]{:S(2)}, u32[]{:S(2)}) async-start(bf16[16,128,128]{2,1,0:T(8,128)(2,1)} %bitcast.21), calls=%async_computation.4 | async-start | bytes 1048576 | tf_op jit(solution)/shard_map/all_to_all | solution.py:123
  165.7 14.1 %all-to-all-start.5 = ((bf16[16,128,128]{2,1,0:T(8,128)(2,1)}), bf16[16,128,128]{2,1,0:T(8,128)(2,1)S(1)}, u32[]{:S(2)}, u32[]{:S(2)}) async-start(bf16[16,128,128]{2,1,0:T(8,128)(2,1)} %bitcast.149), calls=%async_computation.5 | async-start | bytes 1048576 | tf_op jit(solution)/shard_map/all_to_all | solution.py:144
  179.8 14.8 %all-to-all-start.6 = ((bf16[16,128,128]{2,1,0:T(8,128)(2,1)}), bf16[16,128,128]{2,1,0:T(8,128)(2,1)S(1)}, u32[]{:S(2)}, u32[]{:S(2)}) async-start(bf16[16,128,128]{2,1,0:T(8,128)(2,1)} %constant_dynamic-update-slice_fusion.1), calls=%async_computation.6 | async-start | bytes 1048576 | tf_op jit(solution)/shard_map/all_to_all | solution.py:133
  186.1 7.8 %collective-permute-start.3 = (f32[1,256,128]{2,1,0:T(8,128)S(1)}, f32[1,256,128]{2,1,0:T(8,128)S(1)}, u32[]{:S(2)}, u32[]{:S(2)}) collective-permute-start(f32[1,256,128]{2,1,0:T(8,128)S(1)} %slice.119), channel_id=1, source_target_pairs={{16,0},{32,16},{48,32},{64,48},{80,64},{96,80},{112,96},{128,112},... | collective-permute-start | bytes 393224 | tf_op jit(solution)/shard_map/ppermute | solution.py:14
  194.6 18.6 %all-to-all-start.7 = ((bf16[16,128,128]{2,1,0:T(8,128)(2,1)}), bf16[16,128,128]{2,1,0:T(8,128)(2,1)S(1)}, u32[]{:S(2)}, u32[]{:S(2)}) async-start(bf16[16,128,128]{2,1,0:T(8,128)(2,1)} %bitcast.31), calls=%async_computation.7 | async-start | bytes 1048576 | tf_op jit(solution)/shard_map/all_to_all | solution.py:146
  (3 other events, 4.8 us)
